TPU v7x, 256 devices: a whole 4x4x8 slice. The times are simulated.
256 devices in a mesh: pts: 128 (over y, z, x), sta: 2 (over core).
Axes of the slice: x: 4, y: 4, z: 8, core: 2. Of those that a mesh axis runs over, the one named last changes fastest.
Arguments:
- greens: bfloat16 [2, 512, 262144], P(None, 'sta', 'pts'), may hold values from -6 to 6
- source: float32 [262144], P('pts'), may hold values from 0.2 to 5
- observed: float32 [2, 512, 512], P(None, None, 'sta'), may hold values from -12 to 12
- pair_mask: int32 [512, 512], P(None, 'sta'), may hold values 0 or 1
- block_ids: int32 [512], replicated, may hold values from 0 to 31
Outputs:
- kernel: float32 [262144], P('pts')
- adjoint: bfloat16 [2, 512, 512], P(None, None, 'sta')
All inputs are finite; a program needn't handle non-finite values. No bound on the sum of `pair_mask` on one device may be relied on, other than what follows from the above.
Results may differ from a plain program's by a relative error of at most 0.0046.
Values may be sent and summed in bfloat16 or wider, within the bound.
A program may use at most 64 MiB of HBM per device.

v0:
```python
import jax
import jax.numpy as jnp
from jax import lax
from jax.sharding import PartitionSpec as P


def contract_last(left, right):
    return lax.dot_general(
        left, right, (((1,), (1,)), ((), ())), preferred_element_type=jnp.float32
    )


def contract_first(left, right):
    return lax.dot_general(
        left, right, (((0,), (0,)), ((), ())), preferred_element_type=jnp.float32
    )


def body(greens, source, observed, pair_mask, block_ids):
    own_count = greens.shape[1]
    points = greens.shape[2]
    norm_factor = float(points * lax.axis_size("pts")) ** (-0.5)
    weighted = (source[None, None, :] * greens.astype(jnp.float32)).astype(jnp.bfloat16)
    everyone = lax.all_gather(greens, "sta", axis=1, tiled=True)
    corr_real = norm_factor * (
        contract_last(everyone[0], weighted[0]) + contract_last(everyone[1], weighted[1])
    )
    corr_imag = norm_factor * (
        contract_last(everyone[1], weighted[0]) - contract_last(everyone[0], weighted[1])
    )
    partial_value = jnp.stack([corr_real, corr_imag])
    own_groups = lax.dynamic_slice_in_dim(
        block_ids, lax.axis_index("sta") * own_count, own_count, 0
    )
    retained = ((pair_mask == 1) & (block_ids[:, None] != own_groups[None, :])).astype(jnp.float32)
    summed = lax.psum(partial_value, "pts")
    adjoint = (retained[None] * (summed - observed)).astype(jnp.bfloat16)
    wave_real = contract_first(adjoint[0], everyone[0]) + contract_first(adjoint[1], everyone[1])
    wave_imag = contract_first(adjoint[0], everyone[1]) - contract_first(adjoint[1], everyone[0])
    partial_kernel = norm_factor * jnp.sum(
        wave_real * greens[0].astype(jnp.float32) + wave_imag * greens[1].astype(jnp.float32),
        axis=0,
    )
    kernel = lax.psum(partial_kernel, "sta")
    return (kernel, adjoint)


def solution(mesh):
    placed = (P(None, "sta", "pts"), P("pts"), P(None, None, "sta"), P(None, "sta"), P())
    return jax.shard_map(
        body,
        mesh=mesh,
        in_specs=placed,
        out_specs=(P("pts"), P(None, None, "sta")),
        check_vma=False,
    )
```

profile of v0, /device:TPU:1, one launch (start us, length us, event | category | flops | bytes accessed | tf_op | source)
XLA Modules:
  0.0 281.4 jit_solution(3967475922599551682)
XLA Ops:
  7.2 0.0 copy-start
  7.2 0.0 all-gather.2.cloned.1.call-start
  7.2 0.7 all-gather.2.cloned.1.call-update
  7.9 0.0 all-reduce.2.cloned.1.call-start
  8.0 0.8 copy-done
  8.8 2.4 multiply_convert_fusion
  11.2 22.2 %all-gather.2.cloned.1.call-done = bf16[2,512,2048]{2,1,0:T(8,128)(2,1)} async-done(((bf16[2,256,2048]{2,1,0:T(8,128)(2,1)}), bf16[2,512,2048]{2,1,0:T(8,128)(2,1)}) %all-gather.2.cloned.1.call-update) | async-done | bytes 4194320 | tf_op jit(solution)/shard_map/all_gather | solution.py:24
  33.4 2.8 fusion.6
  36.2 0.3 copy-done.1
  36.5 2.3 fusion.5
  38.8 0.0 copy-done.3
  38.8 0.8 fusion.12
  39.6 0.7 fusion.15
  40.3 0.0 copy-start.5
  40.3 0.0 copy-start.4
  40.3 1.1 pad_maximum_fusion
  41.4 0.0 all-reduce.2.cloned.1.call-update
  41.4 0.0 copy-done.5
  41.4 0.1 dynamic_slice.3
  41.5 0.0 copy-done.4
  41.5 0.1 and_convert_fusion
  41.7 0.2 copy.7
  41.9 2.6 copy.8
  44.4 214.1 %all-reduce.2.cloned.1.call-done = f32[2,512,256]{1,2,0:T(8,128)} async-done(((f32[2,512,256]{1,2,0:T(8,128)}), f32[2,512,256]{1,2,0:T(8,128)}) %all-reduce.2.cloned.1.call-update) | async-done | bytes 1048592 | tf_op jit(solution)/shard_map/psum | solution.py:36
  258.5 1.8 multiply_convert_fusion.1
  260.4 1.0 copy.9
  261.4 2.4 fusion.7
  263.8 0.4 copy-done.2
  264.2 0.7 fusion.4
  264.9 0.8 fusion
  265.7 0.9 fusion.3
  266.5 8.0 %psum.15 = f32[2048]{0:T(1024)} all-reduce(f32[2048]{0:T(1024)S(1)} %broadcast_multiply_fusion), channel_id=1, replica_groups=mesh['pts'=128,'sta'=2] {'sta'}, use_global_device_ids=true, to_apply=%region_2.0 | all-reduce | flops 2048 | bytes 16384 | tf_op jit(solution)/shard_map/psum | solution.py:44
  (4 shorter events, 0.0 us)
Async XLA Ops:
  7.2 1.6 copy-start
  7.2 26.2 %all-gather.2.cloned.1.call-start = ((), (), s32[]{:S(2)}) async-start(), calls=%async_computation | async-start | bytes 6291456 | tf_op jit(solution)/shard_map/all_gather | solution.py:24
  7.9 250.6 %all-reduce.2.cloned.1.call-start = ((), (), s32[]{:S(2)}) async-start(), calls=%async_computation.1 | async-start | bytes 2097152 | tf_op jit(solution)/shard_map/psum | solution.py:36
  33.4 3.1 %copy-start.1 = (bf16[2,512,2048]{2,1,0:T(8,128)(2,1)S(1)}, bf16[2,512,2048]{2,1,0:T(8,128)(2,1)}, u32[]{:S(2)}) copy-start(bf16[2,512,2048]{2,1,0:T(8,128)(2,1)} %all-gather.2.cloned.1.call-done) | copy-start | bytes 12582916
  36.5 2.3 copy-start.3
  40.3 1.1 copy-start.5
  40.3 1.2 copy-start.4
  261.4 2.8 %copy-start.2 = (bf16[2,512,2048]{2,1,0:T(8,128)(2,1)S(1)}, bf16[2,512,2048]{2,1,0:T(8,128)(2,1)}, u32[]{:S(2)}) copy-start(bf16[2,512,2048]{2,1,0:T(8,128)(2,1)} %all-gather.2.cloned.1.call-done) | copy-start | bytes 12582916
Sparse Core Ops, SparseCore 0:
  9.8 23.5 all-gather.1
  41.5 216.9 all-reduce.1
where the time goes:
time: 282 us; the launch traced here: 281 us
  waiting for transfers between devices  237 us (84%)
  between operations  14.2 us (5%)
  matrix products  11.3 us (4%)
  blocking collectives  8 us (3%)
  other arithmetic  5.49 us (2%)
  local copies, waits for them, and re-layouts  5.36 us (2%)
    psum x1, waiting for transfers between devices, body(): summed = lax.psum(partial_value, 'pts')  214 us
    all_gather x1, waiting for transfers between devices, body(): everyone = lax.all_gather(greens, 'sta', axis=1, tiled=True)  22.2 us
    psum x1, blocking collectives, body(): kernel = lax.psum(partial_kernel, 'sta')  8 us
    dot_general x4, matrix products, contract_last(): lax.dot_general(left, right, (((1,), (1,)), ((), ())), preferred_element_...  6.56 us
  transfers between devices with their start and end apart: 2, of which 2 were waited for; matrix products, arithmetic and copies ran while one was open for 2% of the time, Pallas kernels for 0%

commit v1 on v0

v1 whole, which is shorter than its diff:
```python
import functools

import jax
import jax.numpy as jnp
from jax import lax
from jax.experimental import pallas as pl
from jax.experimental.pallas import tpu as pltpu
from jax.sharding import PartitionSpec as P

NY, NZ, NX = 4, 8, 4
PLANE = NY * NX
HALF = 256
ROWS = 16
LANES = 128
MESH = pl.DeviceIdType.MESH


def dot_nt(left, right):
    return lax.dot_general(
        left, right, (((1,), (1,)), ((), ())), preferred_element_type=jnp.float32
    )


def dot_nn(left, right):
    return lax.dot_general(
        left, right, (((1,), (0,)), ((), ())), preferred_element_type=jnp.float32
    )


def kernel_body(
    norm_factor,
    greens_ref,
    source_ref,
    observed_ref,
    mask_ref,
    ids_ref,
    kernel_ref,
    adjoint_ref,
    g_all,
    weighted,
    part_buf,
    rs1_buf,
    rs2_send,
    rs2_buf,
    adj,
    adj_t,
    obs_buf,
    mask_buf,
    k_own,
    k_other,
    local_sem,
    gx_send,
    gx_recv,
    rs1_send_sem,
    rs1_recv_sem,
    rs2_send_sem,
    rs2_recv_sem,
    ag1_send_sem,
    ag1_recv_sem,
    ag2_send_sem,
    ag2_recv_sem,
    kx_send,
    kx_recv,
):
    points = greens_ref.shape[2]
    me = lax.axis_index("pts")
    c = lax.axis_index("sta")
    other = 1 - c
    x = me % NX
    z = (me // NX) % NZ
    y = me // (NX * NZ)
    k = y * NX + x

    def plane_peer(d):
        py = (y + d // NX) % NY
        px = (x + d % NX) % NX
        return py * NX + px, (py * NZ + z) * NX + px

    def line_peer(d):
        pz = (z + d) % NZ
        return pz, (y * NZ + pz) * NX + x

    part_z = z // 4
    step_z = (z // 2) % 2
    lanes_z = pl.multiple_of((z % 2) * LANES, LANES)
    half_z = (c + step_z) % 2
    row_k = pl.multiple_of(k * ROWS, ROWS)
    row_z = pl.multiple_of(half_z * HALF + k * ROWS, ROWS)

    load = pltpu.make_async_copy(greens_ref, g_all.at[c], local_sem.at[0])
    load.start()
    load_obs = pltpu.make_async_copy(
        observed_ref.at[part_z, pl.ds(row_z, ROWS), pl.ds(lanes_z, LANES)],
        obs_buf,
        local_sem.at[1],
    )
    load_obs.start()
    load_mask = pltpu.make_async_copy(
        mask_ref.at[pl.ds(row_z, ROWS), pl.ds(lanes_z, LANES)],
        mask_buf,
        local_sem.at[2],
    )
    load_mask.start()

    barrier = pltpu.get_barrier_semaphore()

    def greet_plane(d, carry):
        pl.semaphore_signal(
            barrier, inc=1, device_id=(plane_peer(d)[1], c), device_id_type=MESH
        )
        return carry

    def greet_line(d, carry):
        pl.semaphore_signal(
            barrier, inc=1, device_id=(line_peer(d)[1], c), device_id_type=MESH
        )
        return carry

    pl.semaphore_signal(barrier, inc=1, device_id=(me, other), device_id_type=MESH)
    lax.fori_loop(1, PLANE, greet_plane, 0)
    lax.fori_loop(1, NZ, greet_line, 0)
    pl.semaphore_wait(barrier, 1 + (PLANE - 1) + (NZ - 1))

    exchange = pltpu.make_async_remote_copy(
        src_ref=greens_ref,
        dst_ref=g_all.at[c],
        send_sem=gx_send,
        recv_sem=gx_recv,
        device_id=(me, other),
        device_id_type=MESH,
    )
    exchange.start()

    load.wait()
    source = source_ref[...]
    weighted[0] = (source * g_all[c, 0].astype(jnp.float32)).astype(jnp.bfloat16)
    weighted[1] = (source * g_all[c, 1].astype(jnp.float32)).astype(jnp.bfloat16)

    def rs1_copy(step, d):
        peer, peer_pts = plane_peer(d)
        return pltpu.make_async_remote_copy(
            src_ref=part_buf.at[step, peer],
            dst_ref=rs1_buf.at[step, d],
            send_sem=rs1_send_sem.at[step, d],
            recv_sem=rs1_recv_sem.at[step, d],
            device_id=(peer_pts, c),
            device_id_type=MESH,
        )

    def correlate(step):
        half = (c + step) % 2
        rows_re = g_all[half, 0]
        rows_im = g_all[half, 1]
        real = dot_nt(rows_re, weighted[0]) + dot_nt(rows_im, weighted[1])
        imag = dot_nt(rows_im, weighted[0]) - dot_nt(rows_re, weighted[1])
        shape = (PLANE, ROWS, HALF)
        part_buf[step, :, 0] = (norm_factor * real).astype(jnp.bfloat16).reshape(shape)
        part_buf[step, :, 1] = (norm_factor * imag).astype(jnp.bfloat16).reshape(shape)

        def send(d, carry):
            rs1_copy(step, d).start()
            return carry

        lax.fori_loop(1, PLANE, send, 0)

    correlate(0)
    exchange.wait_recv()
    correlate(1)

    for step in range(2):

        def add(d, total):
            rs1_copy(step, d).wait_recv()
            return total + rs1_buf[step, d].astype(jnp.float32)

        total = lax.fori_loop(1, PLANE, add, part_buf[step, k].astype(jnp.float32))
        for part in range(2):
            for lane in range(2):
                rs2_send[part * 4 + step * 2 + lane] = total[
                    part, :, lane * LANES : (lane + 1) * LANES
                ]

    def rs2_copy(d):
        peer, peer_pts = line_peer(d)
        return pltpu.make_async_remote_copy(
            src_ref=rs2_send.at[peer],
            dst_ref=rs2_buf.at[d],
            send_sem=rs2_send_sem.at[d],
            recv_sem=rs2_recv_sem.at[d],
            device_id=(peer_pts, c),
            device_id_type=MESH,
        )

    def rs2_start(d, carry):
        rs2_copy(d).start()
        return carry

    lax.fori_loop(1, NZ, rs2_start, 0)

    load_obs.wait()
    load_mask.wait()
    ids = ids_ref[...].astype(jnp.float32)
    stations = ids.shape[1]
    spot = lax.broadcasted_iota(jnp.int32, (ROWS, stations), 1)
    row = lax.broadcasted_iota(jnp.int32, (ROWS, stations), 0) + row_z
    row_ids = jnp.sum(jnp.where(spot == row, ids, 0.0), axis=1, keepdims=True)
    col_ids = ids_ref[:, pl.ds(pl.multiple_of(c * HALF + lanes_z, LANES), LANES)].astype(jnp.float32)
    keep = (mask_buf[...] == 1) & (row_ids != col_ids)
    retained = jnp.where(keep, 1.0, 0.0)

    def add_line(d, total):
        rs2_copy(d).wait_recv()
        return total + rs2_buf[d]

    corr = lax.fori_loop(1, NZ, add_line, rs2_send[z])
    block = adj.at[part_z, half_z, pl.ds(row_k, ROWS), pl.ds(lanes_z, LANES)]
    block[...] = (retained * (corr - obs_buf[...])).astype(jnp.bfloat16)

    def ag1_block(d):
        pz = (z - d + NZ) % NZ
        return adj.at[
            pz // 4,
            (c + (pz // 2) % 2) % 2,
            pl.ds(row_k, ROWS),
            pl.ds(pl.multiple_of((pz % 2) * LANES, LANES), LANES),
        ]

    def ag1_start(d, carry):
        pltpu.make_async_remote_copy(
            src_ref=block,
            dst_ref=block,
            send_sem=ag1_send_sem.at[d],
            recv_sem=ag1_recv_sem.at[d],
            device_id=(line_peer(d)[1], c),
            device_id_type=MESH,
        ).start()
        return carry

    def ag1_wait(d, carry):
        arrived = ag1_block(d)
        pltpu.make_async_remote_copy(
            src_ref=arrived,
            dst_ref=arrived,
            send_sem=ag1_send_sem.at[d],
            recv_sem=ag1_recv_sem.at[d],
            device_id=(line_peer(d)[1], c),
            device_id_type=MESH,
        ).wait_recv()
        return carry

    lax.fori_loop(1, NZ, ag1_start, 0)
    lax.fori_loop(1, NZ, ag1_wait, 0)

    def ag2_copy(rows, d):
        return pltpu.make_async_remote_copy(
            src_ref=adj.at[:, :, pl.ds(rows, ROWS), :],
            dst_ref=adj.at[:, :, pl.ds(rows, ROWS), :],
            send_sem=ag2_send_sem.at[d],
            recv_sem=ag2_recv_sem.at[d],
            device_id=(plane_peer(d)[1], c),
            device_id_type=MESH,
        )

    def ag2_start(d, carry):
        ag2_copy(row_k, d).start()
        return carry

    def ag2_wait(d, carry):
        from_y = (y - d // NX + NY) % NY
        from_x = (x - d % NX + NX) % NX
        rows = pl.multiple_of((from_y * NX + from_x) * ROWS, ROWS)
        ag2_copy(rows, d).wait_recv()
        return carry

    lax.fori_loop(1, PLANE, ag2_start, 0)
    lax.fori_loop(1, PLANE, ag2_wait, 0)

    store = pltpu.make_async_copy(adj, adjoint_ref, local_sem.at[3])
    store.start()

    for part in range(2):
        for half in range(2):
            adj_t[part, half] = adj[part, half].T

    width = 512

    @pl.loop(0, points // width)
    def wave(q):
        spots = pl.ds(pl.multiple_of(q * width, width), width)
        real = jnp.zeros((HALF, width), jnp.float32)
        imag = jnp.zeros((HALF, width), jnp.float32)
        for half in range(2):
            g_re = g_all[half, 0, :, spots]
            g_im = g_all[half, 1, :, spots]
            real += dot_nn(adj_t[0, half], g_re) + dot_nn(adj_t[1, half], g_im)
            imag += dot_nn(adj_t[0, half], g_im) - dot_nn(adj_t[1, half], g_re)
        own_re = g_all[c, 0, :, spots].astype(jnp.float32)
        own_im = g_all[c, 1, :, spots].astype(jnp.float32)
        k_own[:, spots] = norm_factor * jnp.sum(
            real * own_re + imag * own_im, axis=0, keepdims=True
        )

    swap = pltpu.make_async_remote_copy(
        src_ref=k_own,
        dst_ref=k_other,
        send_sem=kx_send,
        recv_sem=kx_recv,
        device_id=(me, other),
        device_id_type=MESH,
    )
    swap.start()

    exchange.wait_send()

    def sent_plane(d, carry):
        rs1_copy(0, d).wait_send()
        rs1_copy(1, d).wait_send()
        ag2_copy(row_k, d).wait_send()
        return carry

    def sent_line(d, carry):
        rs2_copy(d).wait_send()
        pltpu.make_async_remote_copy(
            src_ref=block,
            dst_ref=block,
            send_sem=ag1_send_sem.at[d],
            recv_sem=ag1_recv_sem.at[d],
            device_id=(line_peer(d)[1], c),
            device_id_type=MESH,
        ).wait_send()
        return carry

    lax.fori_loop(1, PLANE, sent_plane, 0)
    lax.fori_loop(1, NZ, sent_line, 0)
    swap.wait()
    kernel_ref[...] = k_own[...] + k_other[...]
    store.wait()


def body(greens, source, observed, pair_mask, block_ids):
    own_count, points = greens.shape[1], greens.shape[2]
    stations = observed.shape[1]
    norm_factor = float(points * lax.axis_size("pts")) ** (-0.5)
    vmem = pl.BlockSpec(memory_space=pltpu.VMEM)
    hbm = pl.BlockSpec(memory_space=pl.ANY)
    dma = pltpu.SemaphoreType.DMA
    bf16, f32 = jnp.bfloat16, jnp.float32
    flops = 2 * 2 * 4 * stations * own_count * points
    kernel, adjoint = pl.pallas_call(
        functools.partial(kernel_body, norm_factor),
        out_shape=(
            jax.ShapeDtypeStruct((1, points), f32),
            jax.ShapeDtypeStruct((2, 2, HALF, HALF), bf16),
        ),
        in_specs=[hbm, vmem, hbm, hbm, vmem],
        out_specs=(vmem, hbm),
        scratch_shapes=[
            pltpu.VMEM((2, 2, HALF, points), bf16),
            pltpu.VMEM((2, HALF, points), bf16),
            pltpu.VMEM((2, PLANE, 2, ROWS, HALF), bf16),
            pltpu.VMEM((2, PLANE, 2, ROWS, HALF), bf16),
            pltpu.VMEM((NZ, ROWS, LANES), f32),
            pltpu.VMEM((NZ, ROWS, LANES), f32),
            pltpu.VMEM((2, 2, HALF, HALF), bf16),
            pltpu.VMEM((2, 2, HALF, HALF), bf16),
            pltpu.VMEM((ROWS, LANES), f32),
            pltpu.VMEM((ROWS, LANES), jnp.int32),
            pltpu.VMEM((1, points), f32),
            pltpu.VMEM((1, points), f32),
            dma((4,)),
            dma,
            dma,
            dma((2, PLANE)),
            dma((2, PLANE)),
            dma((NZ,)),
            dma((NZ,)),
            dma((NZ,)),
            dma((NZ,)),
            dma((PLANE,)),
            dma((PLANE,)),
            dma,
            dma,
        ],
        compiler_params=pltpu.CompilerParams(
            collective_id=0, has_side_effects=True, vmem_limit_bytes=48 * 2**20
        ),
        cost_estimate=pl.CostEstimate(
            flops=flops, bytes_accessed=8 * 2**20, transcendentals=0
        ),
        name="noise_kernel",
    )(
        greens,
        source.reshape(1, points),
        observed,
        pair_mask,
        block_ids.reshape(1, stations),
    )
    return kernel.reshape(points), adjoint.reshape(2, stations, own_count)


def solution(mesh):
    placed = (P(None, "sta", "pts"), P("pts"), P(None, None, "sta"), P(None, "sta"), P())
    return jax.shard_map(
        body,
        mesh=mesh,
        in_specs=placed,
        out_specs=(P("pts"), P(None, None, "sta")),
        check_vma=False,
    )
```

time: 282 us -> 52.4 us (0.19)
  waiting for transfers between devices: 237 us -> 0 us
  Pallas kernels: 0 us -> 44.9 us
  between operations: 14.2 us -> 0.65 us
  matrix products: 11.3 us -> 0 us
  blocking collectives: 8 us -> 0 us
  other arithmetic: 5.49 us -> 0 us
    psum x1 -> x0, waiting for transfers between devices: 214 us -> none  [body(): summed = lax.psum(partial_value, 'pts')]
    pallas_call x0 -> x1, Pallas kernels: none -> 44.9 us  [body(): pl.pallas_call(functools.partial(kernel_body, norm_factor), out_shape=(ja...]
    all_gather x1 -> x0, waiting for transfers between devices: 22.2 us -> none  [body(): everyone = lax.all_gather(greens, 'sta', axis=1, tiled=True)]
    dot_general x8 -> x0, matrix products: 11.3 us -> none  [the longest x4 6.56 us: contract_last(): lax.dot_general(left, right, (((1,), (1,)), ((), ())), preferred_element_...]
    psum x1 -> x0, blocking collectives: 8 us -> none  [body(): kernel = lax.psum(partial_kernel, 'sta')]
    convert_element_type x3 -> x0, other arithmetic: 4.41 us -> none  [the longest x1 2.45 us: body(): (source[None, None, :] * greens.astype(jnp.float32)).astype(jnp.bfloat16)]
    unnamed x14 -> x12, local copies, waits for them, and re-layouts: 5.09 us -> 6.62 us
  transfers between devices with their start and end apart: 2 -> 0, of which waited for: 2 -> 0; matrix products, arithmetic and copies ran while one was open for 2% -> 0% of each run, Pallas kernels for 0% -> 0%
where the time goes in v1:
time: 52.4 us; the launch traced here: 52.1 us
  Pallas kernels  44.9 us (86%)
  local copies, waits for them, and re-layouts  6.62 us (13%)
  between operations  0.65 us (1%)
    pallas_call x1, Pallas kernels, body(): pl.pallas_call(functools.partial(kernel_body, norm_factor), out_shape=(ja...  44.9 us
    unnamed x12, local copies, waits for them, and re-layouts  6.62 us

profile of v1, /device:TPU:1, one launch (start us, length us, event | category | flops | bytes accessed | tf_op | source)
XLA Modules:
  0.0 52.1 jit_solution(11124774318834511513)
XLA Ops:
  0.6 0.0 copy-start
  0.6 1.6 %copy-done = bf16[2,256,2048]{2,1,0:T(8,128)(2,1)S(1)} copy-done((bf16[2,256,2048]{2,1,0:T(8,128)(2,1)S(1)}, bf16[2,256,2048]{2,1,0:T(8,128)(2,1)}, u32[]{:S(2)}) %copy-start) | copy-done | bytes 2097176
  2.2 0.0 copy-start.1
  2.2 1.2 %copy-done.1 = f32[2,512,256]{2,1,0:T(8,128)S(1)} copy-done((f32[2,512,256]{2,1,0:T(8,128)S(1)}, f32[2,512,256]{2,1,0:T(8,128)}, u32[]{:S(2)}) %copy-start.1) | copy-done | bytes 1048600
  3.4 0.0 copy-start.2
  3.5 1.0 %copy-done.2 = s32[512,256]{1,0:T(8,128)S(1)} copy-done((s32[512,256]{1,0:T(8,128)S(1)}, s32[512,256]{1,0:T(8,128)}, u32[]{:S(2)}) %copy-start.2) | copy-done | bytes 524312
  4.5 0.0 copy-start.3
  4.5 0.7 %copy-done.3 = f32[2048]{0:T(1024)S(1)} copy-done((f32[2048]{0:T(1024)S(1)}, f32[2048]{0:T(1024)}, u32[]{:S(2)}) %copy-start.3) | copy-done | bytes 8216
  5.2 0.0 copy-start.4
  5.2 0.7 %copy-done.4 = s32[512]{0:T(512)S(1)} copy-done((s32[512]{0:T(512)S(1)}, s32[512]{0:T(512)}, u32[]{:S(2)}) %copy-start.4) | copy-done | bytes 2072
  5.9 44.9 %noise_kernel.1 = (f32[1,2048]{1,0:T(1,128)S(1)}, bf16[2,2,256,256]{3,2,1,0:T(8,128)(2,1)S(1)}) custom-call(bf16[2,256,2048]{2,1,0:T(8,128)(2,1)S(1)} %copy-done, f32[1,2048]{1,0:T(1,128)S(1)} %bitcast.6, f32[2,512,256]{2,1,0:T(8,128)S(1)} %copy-done.1, s32[512,256]{1,0:T(8,128)S(1)} %copy-done.2, s32[1,512]{1,0:T(1,128)S(1)} %bitcast.7), custom_call_target="tpu_custom_call" | custom-call | flops 4294967296 | bytes 8388608 | tf_op jit(solution)/shard_map/noise_kernel/pallas_call | solution.py:349
  50.7 0.6 %copy.9 = f32[2048]{0:T(1024)} copy(f32[2048]{0:T(1024)S(1)} %bitcast.5) | data formatting | bytes 16384
  51.3 0.8 %copy.10 = bf16[2,512,256]{2,1,0:T(8,128)(2,1)} copy(bf16[2,512,256]{2,1,0:T(8,128)(2,1)S(1)} %bitcast.4) | data formatting | bytes 1048576
Async XLA Ops:
  0.6 1.6 %copy-start = (bf16[2,256,2048]{2,1,0:T(8,128)(2,1)S(1)}, bf16[2,256,2048]{2,1,0:T(8,128)(2,1)}, u32[]{:S(2)}) copy-start(bf16[2,256,2048]{2,1,0:T(8,128)(2,1)} %greens_ref.1) | copy-start | bytes 6291460
  2.2 1.2 %copy-start.1 = (f32[2,512,256]{2,1,0:T(8,128)S(1)}, f32[2,512,256]{2,1,0:T(8,128)}, u32[]{:S(2)}) copy-start(f32[2,512,256]{2,1,0:T(8,128)} %observed_ref.1) | copy-start | bytes 3145732
  3.4 1.0 %copy-start.2 = (s32[512,256]{1,0:T(8,128)S(1)}, s32[512,256]{1,0:T(8,128)}, u32[]{:S(2)}) copy-start(s32[512,256]{1,0:T(8,128)} %mask_ref.1) | copy-start | bytes 1572868
  4.5 0.7 %copy-start.3 = (f32[2048]{0:T(1024)S(1)}, f32[2048]{0:T(1024)}, u32[]{:S(2)}) copy-start(f32[2048]{0:T(1024)} %param.6) | copy-start | bytes 24580
  5.2 0.7 %copy-start.4 = (s32[512]{0:T(512)S(1)}, s32[512]{0:T(512)}, u32[]{:S(2)}) copy-start(s32[512]{0:T(512)} %param.9) | copy-start | bytes 6148

commit v2 on v0

v2 whole, which is shorter than its diff:
```python
import functools

import jax
import jax.numpy as jnp
from jax import lax
from jax.experimental import pallas as pl
from jax.experimental.pallas import tpu as pltpu
from jax.sharding import PartitionSpec as P

NY, NZ, NX = 4, 8, 4
PLANE = NY * NX
HALF = 256
SUB = 128
ROWS = 16
GROUPS = SUB // ROWS
WIDTH = 512
CHUNKS = ((0, 0, 2), (1, 0, 1), (1, 1, 1))
MESH = pl.DeviceIdType.MESH


def dot_nt(left, right):
    return lax.dot_general(
        left, right, (((1,), (1,)), ((), ())), preferred_element_type=jnp.float32
    )


def dot_nn(left, right):
    return lax.dot_general(
        left, right, (((1,), (0,)), ((), ())), preferred_element_type=jnp.float32
    )


def kernel_body(
    norm_factor,
    greens_ref,
    source_hbm,
    observed_ref,
    mask_ref,
    ids_hbm,
    kernel_ref,
    adjoint_ref,
    g_all,
    weighted,
    adj,
    obs_buf,
    mask_buf,
    kept,
    source_ref,
    ids_ref,
    k_acc,
    k_own,
    k_other,
    local_sem,
    gx_send,
    gx_recv,
    rs_send,
    rs_recv,
    zx_send,
    zx_recv,
    ag_send,
    ag_recv,
    kx_send,
    kx_recv,
    *buffers,
):
    count = len(CHUNKS)
    part_bufs = buffers[:count]
    rs_bufs = buffers[count : 2 * count]
    zx_bufs = buffers[2 * count :]
    points = greens_ref.shape[2]
    me = lax.axis_index("pts")
    c = lax.axis_index("sta")
    other = 1 - c
    x = me % NX
    z = (me // NX) % NZ
    y = me // (NX * NZ)
    k = y * NX + x
    part_k = k // GROUPS
    row_k = pl.multiple_of((k % GROUPS) * ROWS, ROWS)

    def plane_peer(d):
        py = (y + d // NX) % NY
        px = (x + d % NX) % NX
        return py * NX + px, (py * NZ + z) * NX + px

    def line_peer(d):
        pz = (z + d) % NZ
        return pz, (y * NZ + pz) * NX + x

    def each(start, stop, step):
        def once(d, carry):
            step(d)
            return carry

        lax.fori_loop(start, stop, once, 0)

    load = pltpu.make_async_copy(greens_ref, g_all.at[c], local_sem.at[0])
    load.start()
    load_source = pltpu.make_async_copy(source_hbm, source_ref, local_sem.at[1])
    load_source.start()

    barrier = pltpu.get_barrier_semaphore()

    def greet(pts, sta):
        pl.semaphore_signal(barrier, inc=1, device_id=(pts, sta), device_id_type=MESH)

    greet(me, other)
    each(1, PLANE, lambda d: greet(plane_peer(d)[1], c))
    each(1, NZ, lambda d: greet(line_peer(d)[1], c))
    pl.semaphore_wait(barrier, 1 + (PLANE - 1) + (NZ - 1))

    def exchange(sub):
        rows = pl.ds(sub * SUB, SUB)
        return pltpu.make_async_remote_copy(
            src_ref=greens_ref.at[:, rows, :],
            dst_ref=g_all.at[c, :, rows, :],
            send_sem=gx_send.at[sub],
            recv_sem=gx_recv.at[sub],
            device_id=(me, other),
            device_id_type=MESH,
        )

    for sub in range(2):
        exchange(sub).start()

    load_ids = pltpu.make_async_copy(ids_hbm, ids_ref, local_sem.at[2])
    load_ids.start()
    load_obs = pltpu.make_async_copy(
        observed_ref.at[part_k, :, :, pl.ds(row_k, ROWS), :], obs_buf, local_sem.at[3]
    )
    load_obs.start()
    load_mask = pltpu.make_async_copy(
        mask_ref.at[:, :, pl.ds(row_k, ROWS), :], mask_buf, local_sem.at[4]
    )
    load_mask.start()

    load_source.wait()
    load.wait()
    source = source_ref[...]
    weighted[0] = (source * g_all[c, 0].astype(jnp.float32)).astype(jnp.bfloat16)
    weighted[1] = (source * g_all[c, 1].astype(jnp.float32)).astype(jnp.bfloat16)

    def rs_copy(chunk, d):
        peer, peer_pts = plane_peer(d)
        return pltpu.make_async_remote_copy(
            src_ref=part_bufs[chunk].at[peer],
            dst_ref=rs_bufs[chunk].at[d],
            send_sem=rs_send.at[chunk, d],
            recv_sem=rs_recv.at[chunk, d],
            device_id=(peer_pts, c),
            device_id_type=MESH,
        )

    def zx_copy(chunk, d, slot):
        return pltpu.make_async_remote_copy(
            src_ref=zx_bufs[chunk].at[slot],
            dst_ref=zx_bufs[chunk].at[slot],
            send_sem=zx_send.at[chunk, d],
            recv_sem=zx_recv.at[chunk, d],
            device_id=(line_peer(d)[1], c),
            device_id_type=MESH,
        )

    def half_of(chunk):
        return (c + CHUNKS[chunk][0]) % 2

    def ag_copy(chunk, d, owner):
        _, first, subs = CHUNKS[chunk]
        rows = pl.multiple_of((owner % GROUPS) * ROWS, ROWS)
        block = adj.at[
            owner // GROUPS, half_of(chunk), pl.ds(first, subs), pl.ds(rows, ROWS), :
        ]
        return pltpu.make_async_remote_copy(
            src_ref=block,
            dst_ref=block,
            send_sem=ag_send.at[chunk, d],
            recv_sem=ag_recv.at[chunk, d],
            device_id=(plane_peer(d)[1], c),
            device_id_type=MESH,
        )

    def correlate(chunk):
        _, first, subs = CHUNKS[chunk]
        rows = pl.ds(first * SUB, subs * SUB)
        rows_re = g_all[half_of(chunk), 0, rows, :]
        rows_im = g_all[half_of(chunk), 1, rows, :]
        real = dot_nt(rows_re, weighted[0]) + dot_nt(rows_im, weighted[1])
        imag = dot_nt(rows_im, weighted[0]) - dot_nt(rows_re, weighted[1])
        for part, value in enumerate((real, imag)):
            for sub in range(subs):
                block = value[sub * SUB : (sub + 1) * SUB].astype(jnp.bfloat16)
                part_bufs[chunk][part * GROUPS : (part + 1) * GROUPS, sub] = block.reshape(
                    GROUPS, ROWS, HALF
                )
        each(1, PLANE, lambda d: rs_copy(chunk, d).start())

    def reduce_plane(chunk):
        def add(d, total):
            rs_copy(chunk, d).wait_recv()
            return total + rs_bufs[chunk][d].astype(jnp.float32)

        total = lax.fori_loop(1, PLANE, add, part_bufs[chunk][k].astype(jnp.float32))
        zx_bufs[chunk][z] = total.astype(jnp.bfloat16)
        each(1, NZ, lambda d: zx_copy(chunk, d, z).start())

    def make_adjoint(chunk):
        _, first, subs = CHUNKS[chunk]
        each(1, NZ, lambda d: zx_copy(chunk, d, (z - d + NZ) % NZ).wait_recv())
        half = half_of(chunk)
        corr = zx_bufs[chunk][0].astype(jnp.float32)
        for slot in range(1, NZ):
            corr = corr + zx_bufs[chunk][slot].astype(jnp.float32)
        for sub in range(subs):
            value = kept[half, first + sub] * (
                norm_factor * corr[sub] - obs_buf[half, first + sub]
            )
            adj[part_k, half, first + sub, pl.ds(row_k, ROWS), :] = value.astype(
                jnp.bfloat16
            )
        each(1, PLANE, lambda d: ag_copy(chunk, d, k).start())

    def gather(chunk):
        def wait(d):
            from_y = (y - d // NX + NY) % NY
            from_x = (x - d % NX + NX) % NX
            ag_copy(chunk, d, from_y * NX + from_x).wait_recv()

        each(1, PLANE, wait)

    def store(chunk):
        _, first, subs = CHUNKS[chunk]
        half = half_of(chunk)
        return pltpu.make_async_copy(
            adj.at[:, half, pl.ds(first, subs)],
            adjoint_ref.at[:, half, pl.ds(first, subs)],
            local_sem.at[5 + chunk],
        )

    def swap(piece):
        spots = pl.ds(piece * WIDTH, WIDTH)
        return pltpu.make_async_remote_copy(
            src_ref=k_own.at[:, spots],
            dst_ref=k_other.at[:, spots],
            send_sem=kx_send.at[piece],
            recv_sem=kx_recv.at[piece],
            device_id=(me, other),
            device_id_type=MESH,
        )

    def wave(chunk):
        _, first, subs = CHUNKS[chunk]
        half = half_of(chunk)
        count_rows = subs * SUB
        rows = pl.ds(first * SUB, count_rows)
        res_re = adj[0, half, first : first + subs].reshape(count_rows, HALF)
        res_im = adj[1, half, first : first + subs].reshape(count_rows, HALF)
        for piece in range(points // WIDTH):
            spots = pl.ds(piece * WIDTH, WIDTH)
            own_re = g_all[c, 0, :, spots]
            own_im = g_all[c, 1, :, spots]
            real = dot_nn(res_re, own_re) - dot_nn(res_im, own_im)
            imag = dot_nn(res_re, own_im) + dot_nn(res_im, own_re)
            row_re = g_all[half, 0, rows, spots].astype(jnp.float32)
            row_im = g_all[half, 1, rows, spots].astype(jnp.float32)
            terms = real * row_re + imag * row_im
            terms = jnp.sum(terms.reshape(count_rows // 8, 8, WIDTH), axis=0)
            if chunk > 0:
                terms = terms + k_acc[:, spots]
            if chunk < count - 1:
                k_acc[:, spots] = terms
            else:
                k_own[:, spots] = norm_factor * jnp.sum(terms, axis=0, keepdims=True)
                swap(piece).start()

    correlate(0)
    for chunk in range(1, count):
        exchange(CHUNKS[chunk][1]).wait_recv()
        correlate(chunk)

    load_ids.wait()
    load_mask.wait()
    load_obs.wait()
    ids = ids_ref[...].astype(jnp.float32)
    stations = ids.shape[1]
    col_ids = ids_ref[:, pl.ds(pl.multiple_of(c * HALF, HALF), HALF)].astype(jnp.float32)
    spot = lax.broadcasted_iota(jnp.int32, (ROWS, stations), 1)
    row = lax.broadcasted_iota(jnp.int32, (ROWS, stations), 0) + row_k
    for half in range(2):
        for sub in range(2):
            here = spot == row + (half * HALF + sub * SUB)
            row_ids = jnp.sum(jnp.where(here, ids, 0.0), axis=1, keepdims=True)
            keep = (mask_buf[half, sub] == 1) & (row_ids != col_ids)
            kept[half, sub] = jnp.where(keep, 1.0, 0.0)

    for chunk in range(count):
        reduce_plane(chunk)
    for sub in range(2):
        exchange(sub).wait_send()
    for chunk in range(count):
        make_adjoint(chunk)
    for chunk in range(count):
        each(1, PLANE, lambda d: rs_copy(chunk, d).wait_send())
        each(1, NZ, lambda d: zx_copy(chunk, d, z).wait_send())
    for chunk in range(count):
        gather(chunk)
        store(chunk).start()
        wave(chunk)

    for chunk in range(count):
        each(1, PLANE, lambda d: ag_copy(chunk, d, k).wait_send())
        store(chunk).wait()
    for piece in range(points // WIDTH):
        swap(piece).wait()
    kernel_ref[...] = k_own[...] + k_other[...]


def body(greens, source, observed, pair_mask, block_ids):
    own_count, points = greens.shape[1], greens.shape[2]
    stations = observed.shape[1]
    norm_factor = float(points * lax.axis_size("pts")) ** (-0.5)
    vmem = pl.BlockSpec(memory_space=pltpu.VMEM)
    hbm = pl.BlockSpec(memory_space=pltpu.HBM)
    anywhere = pl.BlockSpec(memory_space=pl.ANY)
    dma = pltpu.SemaphoreType.DMA
    bf16, f32 = jnp.bfloat16, jnp.float32
    count = len(CHUNKS)
    pieces = points // WIDTH

    def blocks(slots):
        return [pltpu.VMEM((slots, subs, ROWS, HALF), bf16) for _, _, subs in CHUNKS]

    operands = (
        greens,
        source.reshape(1, points),
        observed.reshape(2, 2, 2, SUB, HALF),
        pair_mask.reshape(2, 2, SUB, HALF),
        block_ids.reshape(1, stations),
    )
    kernel, adjoint = pl.pallas_call(
        functools.partial(kernel_body, norm_factor),
        out_shape=(
            jax.ShapeDtypeStruct((1, points), f32),
            jax.ShapeDtypeStruct((2, 2, 2, SUB, HALF), bf16),
        ),
        in_specs=[hbm] * 5,
        out_specs=(vmem, anywhere),
        scratch_shapes=[
            pltpu.VMEM((2, 2, HALF, points), bf16),
            pltpu.VMEM((2, HALF, points), bf16),
            pltpu.VMEM((2, 2, 2, SUB, HALF), bf16),
            pltpu.VMEM((2, 2, ROWS, HALF), f32),
            pltpu.VMEM((2, 2, ROWS, HALF), jnp.int32),
            pltpu.VMEM((2, 2, ROWS, HALF), f32),
            pltpu.VMEM((1, points), f32),
            pltpu.VMEM((1, stations), jnp.int32),
            pltpu.VMEM((8, points), f32),
            pltpu.VMEM((1, points), f32),
            pltpu.VMEM((1, points), f32),
            dma((5 + count,)),
            dma((2,)),
            dma((2,)),
            dma((count, PLANE)),
            dma((count, PLANE)),
            dma((count, NZ)),
            dma((count, NZ)),
            dma((count, PLANE)),
            dma((count, PLANE)),
            dma((pieces,)),
            dma((pieces,)),
            *blocks(PLANE),
            *blocks(PLANE),
            *blocks(NZ),
        ],
        compiler_params=pltpu.CompilerParams(
            collective_id=0, has_side_effects=True, vmem_limit_bytes=48 * 2**20
        ),
        cost_estimate=pl.CostEstimate(
            flops=16 * stations * own_count * points,
            bytes_accessed=8 * 2**20,
            transcendentals=0,
        ),
        name="noise_kernel",
    )(*(pltpu.with_memory_space_constraint(operand, pltpu.HBM) for operand in operands))
    return kernel.reshape(points), adjoint.reshape(2, stations, own_count)


def solution(mesh):
    placed = (P(None, "sta", "pts"), P("pts"), P(None, None, "sta"), P(None, "sta"), P())
    return jax.shard_map(
        body,
        mesh=mesh,
        in_specs=placed,
        out_specs=(P("pts"), P(None, None, "sta")),
        check_vma=False,
    )
```

time: 282 us -> 41.4 us (0.15)
  waiting for transfers between devices: 237 us -> 0 us
  Pallas kernels: 0 us -> 39.2 us
  between operations: 14.2 us -> 0.64 us
  matrix products: 11.3 us -> 0 us
  blocking collectives: 8 us -> 0 us
  other arithmetic: 5.49 us -> 0 us
  local copies, waits for them, and re-layouts: 5.36 us -> 1.39 us
    psum x1 -> x0, waiting for transfers between devices: 214 us -> none  [body(): summed = lax.psum(partial_value, 'pts')]
    pallas_call x0 -> x1, Pallas kernels: none -> 39.2 us  [body(): pl.pallas_call(functools.partial(kernel_body, norm_factor), out_shape=(ja...]
    all_gather x1 -> x0, waiting for transfers between devices: 22.2 us -> none  [body(): everyone = lax.all_gather(greens, 'sta', axis=1, tiled=True)]
    dot_general x8 -> x0, matrix products: 11.3 us -> none  [the longest x4 6.56 us: contract_last(): lax.dot_general(left, right, (((1,), (1,)), ((), ())), preferred_element_...]
    psum x1 -> x0, blocking collectives: 8 us -> none  [body(): kernel = lax.psum(partial_kernel, 'sta')]
    convert_element_type x3 -> x0, other arithmetic: 4.41 us -> none  [the longest x1 2.45 us: body(): (source[None, None, :] * greens.astype(jnp.float32)).astype(jnp.bfloat16)]
    unnamed x14 -> x2, local copies, waits for them, and re-layouts: 5.09 us -> 1.39 us
  transfers between devices with their start and end apart: 2 -> 0, of which waited for: 2 -> 0; matrix products, arithmetic and copies ran while one was open for 2% -> 0% of each run, Pallas kernels for 0% -> 0%
where the time goes in v2:
time: 41.4 us; the launch traced here: 41.3 us
  Pallas kernels  39.2 us (95%)
  local copies, waits for them, and re-layouts  1.39 us (3%)
  between operations  0.64 us (2%)
    pallas_call x1, Pallas kernels, body(): pl.pallas_call(functools.partial(kernel_body, norm_factor), out_shape=(ja...  39.2 us
    unnamed x2, local copies, waits for them, and re-layouts  1.39 us

profile of v2, /device:TPU:1, one launch (start us, length us, event | category | flops | bytes accessed | tf_op | source)
XLA Modules:
  0.0 41.3 jit_solution(1032258868327873919)
XLA Ops:
  0.6 39.2 %noise_kernel.1 = (f32[1,2048]{1,0:T(1,128)S(1)}, bf16[2,2,2,128,256]{4,3,2,1,0:T(8,128)(2,1)S(1)}) custom-call(bf16[2,256,2048]{2,1,0:T(8,128)(2,1)} %greens_ref.1, f32[1,2048]{1,0:T(1,128)} %bitcast.10, f32[2,2,2,128,256]{4,3,2,1,0:T(8,128)} %bitcast.8, s32[2,2,128,256]{3,2,1,0:T(8,128)} %bitcast.9, s32[1,512]{1,0:T(1,128)} %bitcast.11), custom_call_target="tpu_custom_call" | custom-call | flops 4294967296 | bytes 8388608 | tf_op jit(solution)/shard_map/noise_kernel/pallas_call | solution.py:339
  39.9 0.6 %copy.9 = f32[2048]{0:T(1024)} copy(f32[2048]{0:T(1024)S(1)} %bitcast.7) | data formatting | bytes 16384
  40.5 0.8 %copy.10 = bf16[2,512,256]{2,1,0:T(8,128)(2,1)} copy(bf16[2,512,256]{2,1,0:T(8,128)(2,1)S(1)} %bitcast.6) | data formatting | bytes 1048576

commit v3 on v2

--- a/solution.py
+++ b/solution.py
@@ -14,8 +14,14 @@
 ROWS = 16
 GROUPS = SUB // ROWS
 WIDTH = 512
-CHUNKS = ((0, 0, 2), (1, 0, 1), (1, 1, 1))
+CHUNKS = ((0, 0, 2), (1, 0, 2))
+PIECES = 4
 MESH = pl.DeviceIdType.MESH
+PLANE_PEERS = (
+    (2, 2), (3, 2), (2, 3), (1, 2), (2, 1), (0, 2), (2, 0), (3, 1),
+    (1, 3), (3, 3), (1, 1), (3, 0), (0, 3), (1, 0), (0, 1),
+)
+LINE_PEERS = (4, 3, 5, 2, 6, 1, 7)
 
 
 def dot_nt(left, right):
@@ -50,6 +56,7 @@
     k_acc,
     k_own,
     k_other,
+    known,
     local_sem,
     gx_send,
     gx_recv,
@@ -100,28 +107,25 @@
     load_source.start()
 
     barrier = pltpu.get_barrier_semaphore()
-
-    def greet(pts, sta):
-        pl.semaphore_signal(barrier, inc=1, device_id=(pts, sta), device_id_type=MESH)
-
-    greet(me, other)
-    each(1, PLANE, lambda d: greet(plane_peer(d)[1], c))
-    each(1, NZ, lambda d: greet(line_peer(d)[1], c))
-    pl.semaphore_wait(barrier, 1 + (PLANE - 1) + (NZ - 1))
-
-    def exchange(sub):
-        rows = pl.ds(sub * SUB, SUB)
+    ring = [plane_peer(d)[1] for d in range(1, NX)]
+    column = [plane_peer(d * NX)[1] for d in range(1, NY)]
+    beside = [line_peer(d)[1] for d in (1, NZ - 1)]
+    beyond = [line_peer(d)[1] for d in (2, NZ - 2)]
+    pl.semaphore_signal(barrier, inc=1, device_id=(me, other), device_id_type=MESH)
+    for pts in (*ring, *column, *beyond, *beside):
+        pl.semaphore_signal(barrier, inc=1, device_id=(pts, c), device_id_type=MESH)
+
+    def exchange(piece):
+        span = points // PIECES
+        spots = pl.ds(piece * span, span)
         return pltpu.make_async_remote_copy(
-            src_ref=greens_ref.at[:, rows, :],
-            dst_ref=g_all.at[c, :, rows, :],
-            send_sem=gx_send.at[sub],
-            recv_sem=gx_recv.at[sub],
+            src_ref=g_all.at[c, :, :, spots],
+            dst_ref=g_all.at[c, :, :, spots],
+            send_sem=gx_send.at[piece],
+            recv_sem=gx_recv.at[piece],
             device_id=(me, other),
             device_id_type=MESH,
         )
-
-    for sub in range(2):
-        exchange(sub).start()
 
     load_ids = pltpu.make_async_copy(ids_hbm, ids_ref, local_sem.at[2])
     load_ids.start()
@@ -180,19 +184,30 @@
         )
 
     def correlate(chunk):
-        _, first, subs = CHUNKS[chunk]
-        rows = pl.ds(first * SUB, subs * SUB)
-        rows_re = g_all[half_of(chunk), 0, rows, :]
-        rows_im = g_all[half_of(chunk), 1, rows, :]
-        real = dot_nt(rows_re, weighted[0]) + dot_nt(rows_im, weighted[1])
-        imag = dot_nt(rows_im, weighted[0]) - dot_nt(rows_re, weighted[1])
+        half = half_of(chunk)
+        real = jnp.zeros((HALF, HALF), jnp.float32)
+        imag = jnp.zeros((HALF, HALF), jnp.float32)
+        span = points // PIECES
+        for piece in range(PIECES):
+            if chunk > 0:
+                exchange(piece).wait_recv()
+            spots = pl.ds(piece * span, span)
+            rows_re = g_all[half, 0, :, spots]
+            rows_im = g_all[half, 1, :, spots]
+            own_re = weighted[0, :, spots]
+            own_im = weighted[1, :, spots]
+            real += dot_nt(rows_re, own_re) + dot_nt(rows_im, own_im)
+            imag += dot_nt(rows_im, own_re) - dot_nt(rows_re, own_im)
         for part, value in enumerate((real, imag)):
-            for sub in range(subs):
+            for sub in range(2):
                 block = value[sub * SUB : (sub + 1) * SUB].astype(jnp.bfloat16)
                 part_bufs[chunk][part * GROUPS : (part + 1) * GROUPS, sub] = block.reshape(
                     GROUPS, ROWS, HALF
                 )
-        each(1, PLANE, lambda d: rs_copy(chunk, d).start())
+
+    def scatter(chunk, peers=PLANE_PEERS):
+        for dy, dx in peers:
+            rs_copy(chunk, dy * NX + dx).start()
 
     def reduce_plane(chunk):
         def add(d, total):
@@ -201,7 +216,8 @@
 
         total = lax.fori_loop(1, PLANE, add, part_bufs[chunk][k].astype(jnp.float32))
         zx_bufs[chunk][z] = total.astype(jnp.bfloat16)
-        each(1, NZ, lambda d: zx_copy(chunk, d, z).start())
+        for d in LINE_PEERS:
+            zx_copy(chunk, d, z).start()
 
     def make_adjoint(chunk):
         _, first, subs = CHUNKS[chunk]
@@ -217,7 +233,8 @@
             adj[part_k, half, first + sub, pl.ds(row_k, ROWS), :] = value.astype(
                 jnp.bfloat16
             )
-        each(1, PLANE, lambda d: ag_copy(chunk, d, k).start())
+        for dy, dx in PLANE_PEERS:
+            ag_copy(chunk, dy * NX + dx, k).start()
 
     def gather(chunk):
         def wait(d):
@@ -273,9 +290,12 @@
                 swap(piece).start()
 
     correlate(0)
-    for chunk in range(1, count):
-        exchange(CHUNKS[chunk][1]).wait_recv()
-        correlate(chunk)
+    pl.semaphore_wait(barrier, 1 + len(ring) + len(column) + len(beside) + len(beyond))
+    for piece in range(PIECES):
+        exchange(piece).start()
+    for pts in (*ring, *beyond):
+        pl.semaphore_signal(known, inc=1, device_id=(pts, c), device_id_type=MESH)
+    scatter(0, [(dy, dx) for dy, dx in PLANE_PEERS if dy * dx == 0])
 
     load_ids.wait()
     load_mask.wait()
@@ -292,22 +312,31 @@
             keep = (mask_buf[half, sub] == 1) & (row_ids != col_ids)
             kept[half, sub] = jnp.where(keep, 1.0, 0.0)
 
+    pl.semaphore_wait(known, len(ring) + len(beyond))
+    scatter(0, [(dy, dx) for dy, dx in PLANE_PEERS if dy * dx != 0])
+    for chunk in range(1, count):
+        correlate(chunk)
+        scatter(chunk)
     for chunk in range(count):
         reduce_plane(chunk)
-    for sub in range(2):
-        exchange(sub).wait_send()
+    for piece in range(PIECES):
+        exchange(piece).wait_send()
+    for chunk in range(count):
+        each(1, PLANE, lambda d: rs_copy(chunk, d).wait_send())
     for chunk in range(count):
         make_adjoint(chunk)
     for chunk in range(count):
-        each(1, PLANE, lambda d: rs_copy(chunk, d).wait_send())
         each(1, NZ, lambda d: zx_copy(chunk, d, z).wait_send())
     for chunk in range(count):
+        if chunk == count - 1:
+            for sent in range(count - 1):
+                each(1, PLANE, lambda d: ag_copy(sent, d, k).wait_send())
         gather(chunk)
         store(chunk).start()
         wave(chunk)
 
-    for chunk in range(count):
-        each(1, PLANE, lambda d: ag_copy(chunk, d, k).wait_send())
+    each(1, PLANE, lambda d: ag_copy(count - 1, d, k).wait_send())
+    for chunk in range(count):
         store(chunk).wait()
     for piece in range(points // WIDTH):
         swap(piece).wait()
@@ -356,9 +385,10 @@
             pltpu.VMEM((8, points), f32),
             pltpu.VMEM((1, points), f32),
             pltpu.VMEM((1, points), f32),
+            pltpu.SemaphoreType.REGULAR,
             dma((5 + count,)),
-            dma((2,)),
-            dma((2,)),
+            dma((PIECES,)),
+            dma((PIECES,)),
             dma((count, PLANE)),
             dma((count, PLANE)),
             dma((count, NZ)),

time: 41.4 us -> 38.1 us (0.920)
  Pallas kernels: 39.2 us -> 36 us
    pallas_call x1, Pallas kernels: 39.2 us -> 36 us  [body(): pl.pallas_call(functools.partial(kernel_body, norm_factor), out_shape=(ja...]
where the time goes in v3:
time: 38.1 us; the launch traced here: 38 us
  Pallas kernels  36 us (94%)
  local copies, waits for them, and re-layouts  1.39 us (4%)
  between operations  0.64 us (2%)
    pallas_call x1, Pallas kernels, body(): pl.pallas_call(functools.partial(kernel_body, norm_factor), out_shape=(ja...  36 us
    unnamed x2, local copies, waits for them, and re-layouts  1.39 us

profile of v3, /device:TPU:1, one launch (start us, length us, event | category | flops | bytes accessed | tf_op | source)
XLA Modules:
  0.0 38.0 jit_solution(18293901083609879349)
XLA Ops:
  0.6 36.0 %noise_kernel.1 = (f32[1,2048]{1,0:T(1,128)S(1)}, bf16[2,2,2,128,256]{4,3,2,1,0:T(8,128)(2,1)S(1)}) custom-call(bf16[2,256,2048]{2,1,0:T(8,128)(2,1)} %greens_ref.1, f32[1,2048]{1,0:T(1,128)} %bitcast.10, f32[2,2,2,128,256]{4,3,2,1,0:T(8,128)} %bitcast.8, s32[2,2,128,256]{3,2,1,0:T(8,128)} %bitcast.9, s32[1,512]{1,0:T(1,128)} %bitcast.11), custom_call_target="tpu_custom_call" | custom-call | flops 4294967296 | bytes 8388608 | tf_op jit(solution)/shard_map/noise_kernel/pallas_call | solution.py:368
  36.6 0.6 %copy.9 = f32[2048]{0:T(1024)} copy(f32[2048]{0:T(1024)S(1)} %bitcast.7) | data formatting | bytes 16384
  37.2 0.8 %copy.10 = bf16[2,512,256]{2,1,0:T(8,128)(2,1)} copy(bf16[2,512,256]{2,1,0:T(8,128)(2,1)S(1)} %bitcast.6) | data formatting | bytes 1048576

commit v4 on v3

--- a/solution.py
+++ b/solution.py
@@ -57,6 +57,7 @@
     k_own,
     k_other,
     known,
+    load_sem,
     local_sem,
     gx_send,
     gx_recv,
@@ -101,11 +102,6 @@
 
         lax.fori_loop(start, stop, once, 0)
 
-    load = pltpu.make_async_copy(greens_ref, g_all.at[c], local_sem.at[0])
-    load.start()
-    load_source = pltpu.make_async_copy(source_hbm, source_ref, local_sem.at[1])
-    load_source.start()
-
     barrier = pltpu.get_barrier_semaphore()
     ring = [plane_peer(d)[1] for d in range(1, NX)]
     column = [plane_peer(d * NX)[1] for d in range(1, NY)]
@@ -114,6 +110,18 @@
     pl.semaphore_signal(barrier, inc=1, device_id=(me, other), device_id_type=MESH)
     for pts in (*ring, *column, *beyond, *beside):
         pl.semaphore_signal(barrier, inc=1, device_id=(pts, c), device_id_type=MESH)
+
+    def load(piece):
+        span = points // PIECES
+        spots = pl.ds(piece * span, span)
+        return pltpu.make_async_copy(
+            greens_ref.at[:, :, spots], g_all.at[c, :, :, spots], load_sem.at[piece]
+        )
+
+    for piece in range(PIECES):
+        load(piece).start()
+    load_source = pltpu.make_async_copy(source_hbm, source_ref, local_sem.at[1])
+    load_source.start()
 
     def exchange(piece):
         span = points // PIECES
@@ -137,12 +145,6 @@
         mask_ref.at[:, :, pl.ds(row_k, ROWS), :], mask_buf, local_sem.at[4]
     )
     load_mask.start()
-
-    load_source.wait()
-    load.wait()
-    source = source_ref[...]
-    weighted[0] = (source * g_all[c, 0].astype(jnp.float32)).astype(jnp.bfloat16)
-    weighted[1] = (source * g_all[c, 1].astype(jnp.float32)).astype(jnp.bfloat16)
 
     def rs_copy(chunk, d):
         peer, peer_pts = plane_peer(d)
@@ -289,12 +291,18 @@
                 k_own[:, spots] = norm_factor * jnp.sum(terms, axis=0, keepdims=True)
                 swap(piece).start()
 
-    correlate(0)
     pl.semaphore_wait(barrier, 1 + len(ring) + len(column) + len(beside) + len(beyond))
     for piece in range(PIECES):
+        load(piece).wait()
         exchange(piece).start()
     for pts in (*ring, *beyond):
         pl.semaphore_signal(known, inc=1, device_id=(pts, c), device_id_type=MESH)
+    load_source.wait()
+    source = source_ref[...]
+    weighted[0] = (source * g_all[c, 0].astype(jnp.float32)).astype(jnp.bfloat16)
+    weighted[1] = (source * g_all[c, 1].astype(jnp.float32)).astype(jnp.bfloat16)
+
+    correlate(0)
     scatter(0, [(dy, dx) for dy, dx in PLANE_PEERS if dy * dx == 0])
 
     load_ids.wait()
@@ -386,6 +394,7 @@
             pltpu.VMEM((1, points), f32),
             pltpu.VMEM((1, points), f32),
             pltpu.SemaphoreType.REGULAR,
+            dma((PIECES,)),
             dma((5 + count,)),
             dma((PIECES,)),
             dma((PIECES,)),

time: 38.1 us -> 37.8 us (level)
  no operation moved by 1% of the time
where the time goes in v4:
time: 37.8 us; the launch traced here: 37.7 us
  Pallas kernels  35.7 us (94%)
  local copies, waits for them, and re-layouts  1.39 us (4%)
  between operations  0.64 us (2%)
    pallas_call x1, Pallas kernels, body(): pl.pallas_call(functools.partial(kernel_body, norm_factor), out_shape=(ja...  35.7 us
    unnamed x2, local copies, waits for them, and re-layouts  1.39 us

profile of v4, /device:TPU:1, one launch (start us, length us, event | category | flops | bytes accessed | tf_op | source)
XLA Modules:
  0.0 37.7 jit_solution(8727430534634876031)
XLA Ops:
  0.6 35.7 %noise_kernel.1 = (f32[1,2048]{1,0:T(1,128)S(1)}, bf16[2,2,2,128,256]{4,3,2,1,0:T(8,128)(2,1)S(1)}) custom-call(bf16[2,256,2048]{2,1,0:T(8,128)(2,1)} %greens_ref.1, f32[1,2048]{1,0:T(1,128)} %bitcast.10, f32[2,2,2,128,256]{4,3,2,1,0:T(8,128)} %bitcast.8, s32[2,2,128,256]{3,2,1,0:T(8,128)} %bitcast.9, s32[1,512]{1,0:T(1,128)} %bitcast.11), custom_call_target="tpu_custom_call" | custom-call | flops 4294967296 | bytes 8388608 | tf_op jit(solution)/shard_map/noise_kernel/pallas_call | solution.py:376
  36.3 0.6 %copy.9 = f32[2048]{0:T(1024)} copy(f32[2048]{0:T(1024)S(1)} %bitcast.7) | data formatting | bytes 16384
  36.9 0.8 %copy.10 = bf16[2,512,256]{2,1,0:T(8,128)(2,1)} copy(bf16[2,512,256]{2,1,0:T(8,128)(2,1)S(1)} %bitcast.6) | data formatting | bytes 1048576

commit v5 on v4

--- a/solution.py
+++ b/solution.py
@@ -13,7 +13,7 @@
 SUB = 128
 ROWS = 16
 GROUPS = SUB // ROWS
-WIDTH = 512
+WIDTH = 2048
 CHUNKS = ((0, 0, 2), (1, 0, 2))
 PIECES = 4
 MESH = pl.DeviceIdType.MESH
@@ -303,7 +303,6 @@
     weighted[1] = (source * g_all[c, 1].astype(jnp.float32)).astype(jnp.bfloat16)
 
     correlate(0)
-    scatter(0, [(dy, dx) for dy, dx in PLANE_PEERS if dy * dx == 0])
 
     load_ids.wait()
     load_mask.wait()
@@ -321,7 +320,7 @@
             kept[half, sub] = jnp.where(keep, 1.0, 0.0)
 
     pl.semaphore_wait(known, len(ring) + len(beyond))
-    scatter(0, [(dy, dx) for dy, dx in PLANE_PEERS if dy * dx != 0])
+    scatter(0)
     for chunk in range(1, count):
         correlate(chunk)
         scatter(chunk)

time: 37.8 us -> 37.2 us (0.984)
  Pallas kernels: 35.7 us -> 35.1 us
    pallas_call x1, Pallas kernels: 35.7 us -> 35.1 us  [body(): pl.pallas_call(functools.partial(kernel_body, norm_factor), out_shape=(ja...]
where the time goes in v5:
time: 37.2 us; the launch traced here: 37.1 us
  Pallas kernels  35.1 us (94%)
  local copies, waits for them, and re-layouts  1.39 us (4%)
  between operations  0.64 us (2%)
    pallas_call x1, Pallas kernels, body(): pl.pallas_call(functools.partial(kernel_body, norm_factor), out_shape=(ja...  35.1 us
    unnamed x2, local copies, waits for them, and re-layouts  1.39 us

profile of v5, /device:TPU:1, one launch (start us, length us, event | category | flops | bytes accessed | tf_op | source)
XLA Modules:
  0.0 37.1 jit_solution(3946771663122374069)
XLA Ops:
  0.6 35.1 %noise_kernel.1 = (f32[1,2048]{1,0:T(1,128)S(1)}, bf16[2,2,2,128,256]{4,3,2,1,0:T(8,128)(2,1)S(1)}) custom-call(bf16[2,256,2048]{2,1,0:T(8,128)(2,1)} %greens_ref.1, f32[1,2048]{1,0:T(1,128)} %bitcast.10, f32[2,2,2,128,256]{4,3,2,1,0:T(8,128)} %bitcast.8, s32[2,2,128,256]{3,2,1,0:T(8,128)} %bitcast.9, s32[1,512]{1,0:T(1,128)} %bitcast.11), custom_call_target="tpu_custom_call" | custom-call | flops 4294967296 | bytes 8388608 | tf_op jit(solution)/shard_map/noise_kernel/pallas_call | solution.py:375
  35.7 0.6 %copy.9 = f32[2048]{0:T(1024)} copy(f32[2048]{0:T(1024)S(1)} %bitcast.7) | data formatting | bytes 16384
  36.3 0.8 %copy.10 = bf16[2,512,256]{2,1,0:T(8,128)(2,1)} copy(bf16[2,512,256]{2,1,0:T(8,128)(2,1)S(1)} %bitcast.6) | data formatting | bytes 1048576

commit v6 on v5

--- a/solution.py
+++ b/solution.py
@@ -15,7 +15,7 @@
 GROUPS = SUB // ROWS
 WIDTH = 2048
 CHUNKS = ((0, 0, 2), (1, 0, 2))
-PIECES = 4
+PIECES = 8
 MESH = pl.DeviceIdType.MESH
 PLANE_PEERS = (
     (2, 2), (3, 2), (2, 3), (1, 2), (2, 1), (0, 2), (2, 0), (3, 1),
@@ -273,12 +273,18 @@
         rows = pl.ds(first * SUB, count_rows)
         res_re = adj[0, half, first : first + subs].reshape(count_rows, HALF)
         res_im = adj[1, half, first : first + subs].reshape(count_rows, HALF)
+        residual = jnp.concatenate(
+            [
+                jnp.concatenate([res_re, -res_im], axis=1),
+                jnp.concatenate([res_im, res_re], axis=1),
+            ],
+            axis=0,
+        )
         for piece in range(points // WIDTH):
             spots = pl.ds(piece * WIDTH, WIDTH)
-            own_re = g_all[c, 0, :, spots]
-            own_im = g_all[c, 1, :, spots]
-            real = dot_nn(res_re, own_re) - dot_nn(res_im, own_im)
-            imag = dot_nn(res_re, own_im) + dot_nn(res_im, own_re)
+            own = g_all[c, :, :, spots].reshape(2 * HALF, WIDTH)
+            product = dot_nn(residual, own)
+            real, imag = product[:count_rows], product[count_rows:]
             row_re = g_all[half, 0, rows, spots].astype(jnp.float32)
             row_im = g_all[half, 1, rows, spots].astype(jnp.float32)
             terms = real * row_re + imag * row_im

time: 37.2 us -> 37 us (level)
  no operation moved by 1% of the time
where the time goes in v6:
time: 37 us; the launch traced here: 36.9 us
  Pallas kernels  34.8 us (94%)
  local copies, waits for them, and re-layouts  1.39 us (4%)
  between operations  0.64 us (2%)
    pallas_call x1, Pallas kernels, body(): pl.pallas_call(functools.partial(kernel_body, norm_factor), out_shape=(ja...  34.8 us
    unnamed x2, local copies, waits for them, and re-layouts  1.39 us

profile of v6, /device:TPU:1, one launch (start us, length us, event | category | flops | bytes accessed | tf_op | source)
XLA Modules:
  0.0 36.9 jit_solution(4470792759669339313)
XLA Ops:
  0.6 34.8 %noise_kernel.1 = (f32[1,2048]{1,0:T(1,128)S(1)}, bf16[2,2,2,128,256]{4,3,2,1,0:T(8,128)(2,1)S(1)}) custom-call(bf16[2,256,2048]{2,1,0:T(8,128)(2,1)} %greens_ref.1, f32[1,2048]{1,0:T(1,128)} %bitcast.10, f32[2,2,2,128,256]{4,3,2,1,0:T(8,128)} %bitcast.8, s32[2,2,128,256]{3,2,1,0:T(8,128)} %bitcast.9, s32[1,512]{1,0:T(1,128)} %bitcast.11), custom_call_target="tpu_custom_call" | custom-call | flops 4294967296 | bytes 8388608 | tf_op jit(solution)/shard_map/noise_kernel/pallas_call | solution.py:381
  35.5 0.6 %copy.9 = f32[2048]{0:T(1024)} copy(f32[2048]{0:T(1024)S(1)} %bitcast.7) | data formatting | bytes 16384
  36.1 0.8 %copy.10 = bf16[2,512,256]{2,1,0:T(8,128)(2,1)} copy(bf16[2,512,256]{2,1,0:T(8,128)(2,1)S(1)} %bitcast.6) | data formatting | bytes 1048576

commit v7 on v6

--- a/solution.py
+++ b/solution.py
@@ -13,7 +13,7 @@
 SUB = 128
 ROWS = 16
 GROUPS = SUB // ROWS
-WIDTH = 2048
+WIDTH = 1024
 CHUNKS = ((0, 0, 2), (1, 0, 2))
 PIECES = 8
 MESH = pl.DeviceIdType.MESH
@@ -103,13 +103,13 @@
         lax.fori_loop(start, stop, once, 0)
 
     barrier = pltpu.get_barrier_semaphore()
-    ring = [plane_peer(d)[1] for d in range(1, NX)]
-    column = [plane_peer(d * NX)[1] for d in range(1, NY)]
+    ring = [plane_peer(d)[1] for d in (2, 1, 3)]
+    column = [plane_peer(d * NX)[1] for d in (2, 1, 3)]
     beside = [line_peer(d)[1] for d in (1, NZ - 1)]
     beyond = [line_peer(d)[1] for d in (2, NZ - 2)]
+    for pts in (*beyond, *ring, *column, *beside):
+        pl.semaphore_signal(barrier, inc=1, device_id=(pts, c), device_id_type=MESH)
     pl.semaphore_signal(barrier, inc=1, device_id=(me, other), device_id_type=MESH)
-    for pts in (*ring, *column, *beyond, *beside):
-        pl.semaphore_signal(barrier, inc=1, device_id=(pts, c), device_id_type=MESH)
 
     def load(piece):
         span = points // PIECES
@@ -258,8 +258,8 @@
     def swap(piece):
         spots = pl.ds(piece * WIDTH, WIDTH)
         return pltpu.make_async_remote_copy(
-            src_ref=k_own.at[:, spots],
-            dst_ref=k_other.at[:, spots],
+            src_ref=k_own,
+            dst_ref=k_other,
             send_sem=kx_send.at[piece],
             recv_sem=kx_recv.at[piece],
             device_id=(me, other),
@@ -295,7 +295,6 @@
                 k_acc[:, spots] = terms
             else:
                 k_own[:, spots] = norm_factor * jnp.sum(terms, axis=0, keepdims=True)
-                swap(piece).start()
 
     pl.semaphore_wait(barrier, 1 + len(ring) + len(column) + len(beside) + len(beyond))
     for piece in range(PIECES):
@@ -347,12 +346,13 @@
         gather(chunk)
         store(chunk).start()
         wave(chunk)
+        if chunk == count - 1:
+            swap(0).start()
 
     each(1, PLANE, lambda d: ag_copy(count - 1, d, k).wait_send())
     for chunk in range(count):
         store(chunk).wait()
-    for piece in range(points // WIDTH):
-        swap(piece).wait()
+    swap(0).wait()
     kernel_ref[...] = k_own[...] + k_other[...]
 
 

time: 37 us -> 36.9 us (level)
  no operation moved by 1% of the time
where the time goes in v7:
time: 36.9 us; the launch traced here: 36.8 us
  Pallas kernels  34.7 us (94%)
  local copies, waits for them, and re-layouts  1.39 us (4%)
  between operations  0.64 us (2%)
    pallas_call x1, Pallas kernels, body(): pl.pallas_call(functools.partial(kernel_body, norm_factor), out_shape=(ja...  34.7 us
    unnamed x2, local copies, waits for them, and re-layouts  1.39 us

profile of v7, /device:TPU:1, one launch (start us, length us, event | category | flops | bytes accessed | tf_op | source)
XLA Modules:
  0.0 36.8 jit_solution(9733635700114565641)
XLA Ops:
  0.6 34.7 %noise_kernel.1 = (f32[1,2048]{1,0:T(1,128)S(1)}, bf16[2,2,2,128,256]{4,3,2,1,0:T(8,128)(2,1)S(1)}) custom-call(bf16[2,256,2048]{2,1,0:T(8,128)(2,1)} %greens_ref.1, f32[1,2048]{1,0:T(1,128)} %bitcast.10, f32[2,2,2,128,256]{4,3,2,1,0:T(8,128)} %bitcast.8, s32[2,2,128,256]{3,2,1,0:T(8,128)} %bitcast.9, s32[1,512]{1,0:T(1,128)} %bitcast.11), custom_call_target="tpu_custom_call" | custom-call | flops 4294967296 | bytes 8388608 | tf_op jit(solution)/shard_map/noise_kernel/pallas_call | solution.py:381
  35.4 0.6 %copy.9 = f32[2048]{0:T(1024)} copy(f32[2048]{0:T(1024)S(1)} %bitcast.7) | data formatting | bytes 16384
  36.0 0.8 %copy.10 = bf16[2,512,256]{2,1,0:T(8,128)(2,1)} copy(bf16[2,512,256]{2,1,0:T(8,128)(2,1)S(1)} %bitcast.6) | data formatting | bytes 1048576

commit v8 on v6

--- a/solution.py
+++ b/solution.py
@@ -332,12 +332,12 @@
         scatter(chunk)
     for chunk in range(count):
         reduce_plane(chunk)
+    for chunk in range(count):
+        make_adjoint(chunk)
     for piece in range(PIECES):
         exchange(piece).wait_send()
     for chunk in range(count):
         each(1, PLANE, lambda d: rs_copy(chunk, d).wait_send())
-    for chunk in range(count):
-        make_adjoint(chunk)
     for chunk in range(count):
         each(1, NZ, lambda d: zx_copy(chunk, d, z).wait_send())
     for chunk in range(count):

time: 37 us -> 37 us (level)
  no operation moved by 1% of the time
where the time goes in v8:
time: 37 us; the launch traced here: 36.9 us
  Pallas kernels  34.8 us (94%)
  local copies, waits for them, and re-layouts  1.39 us (4%)
  between operations  0.64 us (2%)
    pallas_call x1, Pallas kernels, body(): pl.pallas_call(functools.partial(kernel_body, norm_factor), out_shape=(ja...  34.8 us
    unnamed x2, local copies, waits for them, and re-layouts  1.39 us

profile of v8, /device:TPU:1, one launch (start us, length us, event | category | flops | bytes accessed | tf_op | source)
XLA Modules:
  0.0 36.9 jit_solution(5119632483246605272)
XLA Ops:
  0.6 34.8 %noise_kernel.1 = (f32[1,2048]{1,0:T(1,128)S(1)}, bf16[2,2,2,128,256]{4,3,2,1,0:T(8,128)(2,1)S(1)}) custom-call(bf16[2,256,2048]{2,1,0:T(8,128)(2,1)} %greens_ref.1, f32[1,2048]{1,0:T(1,128)} %bitcast.10, f32[2,2,2,128,256]{4,3,2,1,0:T(8,128)} %bitcast.8, s32[2,2,128,256]{3,2,1,0:T(8,128)} %bitcast.9, s32[1,512]{1,0:T(1,128)} %bitcast.11), custom_call_target="tpu_custom_call" | custom-call | flops 4294967296 | bytes 8388608 | tf_op jit(solution)/shard_map/noise_kernel/pallas_call | solution.py:381
  35.5 0.6 %copy.9 = f32[2048]{0:T(1024)} copy(f32[2048]{0:T(1024)S(1)} %bitcast.7) | data formatting | bytes 16384
  36.1 0.8 %copy.10 = bf16[2,512,256]{2,1,0:T(8,128)(2,1)} copy(bf16[2,512,256]{2,1,0:T(8,128)(2,1)S(1)} %bitcast.6) | data formatting | bytes 1048576
